TPU v7x, 256 devices: a whole 4x4x8 slice. The times are simulated.
256 devices in a mesh: img: 4 (over z_hi), exp: 64 (over x, z_lo, y, core).
Axes of the slice: x: 4, y: 4, z: 8 (z_hi: 4, z_lo: 2; z = z_hi * 2 + z_lo), core: 2. Of those that a mesh axis runs over, the one named last changes fastest.
Arguments:
- tokens: bfloat16 [3072, 64, 1280], P(('img', 'exp')), may hold values from -12 to 12
- router: bfloat16 [1280, 16], replicated, may hold values from -0.2 to 0.2
- grad_out: bfloat16 [3072, 64, 1280], P(('img', 'exp')), may hold values from -6 to 6
- slot_out: bfloat16 [3072, 16, 1280], P(('img', 'exp')), may hold values from -6 to 6
- hidden_pre: bfloat16 [3072, 64, 1280], P('img', 'exp'), may hold values from -6 to 6
- w_in: bfloat16 [64, 1280, 1280], P('exp', 'img'), may hold values from -0.15625 to 0.15625
- w_out: bfloat16 [64, 1280, 1280], P('exp', 'img'), may hold values from -0.078125 to 0.078125
Outputs:
- d_tokens: bfloat16 [3072, 64, 1280], P(('img', 'exp'))
- d_w_in: bfloat16 [64, 1280, 1280], P('exp', 'img')
- d_w_out: bfloat16 [64, 1280, 1280], P('exp', 'img')
- d_router: float32 [1280, 16], replicated
All inputs are finite; a program needn't handle non-finite values.
Results may differ from a plain program's by a relative error of at most 0.015.
Values may be sent and summed in bfloat16 or wider, within the bound.
No kernel may reach another device: no remote copies, remote signals or barrier semaphores. Data moves between devices by JAX's collectives and lax.ppermute only.
A program may use at most 128 MiB of HBM per device.

v0:
```python
import jax
import jax.numpy as jnp
from jax import lax
from jax.sharding import PartitionSpec as P


def gelu_tanh(values):
    return jax.nn.gelu(values, approximate=True)


def on_device(tokens, router, grad_out, slot_out, hidden_pre, w_in, w_out):
    image_count, token_count, model_width = tokens.shape
    slot_count = router.shape[1]
    part_count = lax.axis_size("exp")
    group_size = part_count // slot_count
    logits = jnp.einsum("bmd,ds->bms", tokens, router, preferred_element_type=jnp.float32)
    dispatch = jax.nn.softmax(logits, axis=1)
    combine = jax.nn.softmax(logits, axis=2)
    dispatch_w = dispatch.astype(jnp.bfloat16)
    combine_w = combine.astype(jnp.bfloat16)
    slot_inputs = jnp.einsum(
        "bms,bmd->bsd", dispatch_w, tokens, preferred_element_type=jnp.float32
    ).astype(jnp.bfloat16)
    slot_grads = jnp.einsum(
        "bms,bmd->bsd", combine_w, grad_out, preferred_element_type=jnp.float32
    ).astype(jnp.bfloat16)
    paired = jnp.stack([slot_inputs, slot_grads])
    outgoing = jnp.repeat(paired, group_size, axis=2)
    arrived = lax.all_to_all(outgoing, "exp", split_axis=2, concat_axis=1, tiled=True)
    rows_in = arrived.reshape(2, -1, model_width)
    expert_inputs = rows_in[0]
    expert_grads = rows_in[1]
    pre_values = hidden_pre.reshape(-1, hidden_pre.shape[2]).astype(jnp.float32)
    activation, gelu_back = jax.vjp(gelu_tanh, pre_values)
    activation = activation.astype(jnp.bfloat16)
    hidden_grad = jnp.dot(
        expert_grads,
        lax.all_gather(w_out, "img", axis=1, tiled=True)[0].T,
        preferred_element_type=jnp.float32,
    )
    pre_grad = gelu_back(hidden_grad)[0].astype(jnp.bfloat16)
    partial_value = jnp.dot(
        pre_grad,
        lax.all_gather(w_in, "img", axis=1, tiled=True)[0].T,
        preferred_element_type=jnp.float32,
    )
    columns = expert_inputs
    in_gradient = lax.psum_scatter(
        jnp.dot(columns.T, pre_grad, preferred_element_type=jnp.float32).astype(jnp.bfloat16),
        "img",
        scatter_dimension=0,
        tiled=True,
    )
    columns = activation
    out_gradient = lax.psum_scatter(
        jnp.dot(columns.T, expert_grads, preferred_element_type=jnp.float32).astype(jnp.bfloat16),
        "img",
        scatter_dimension=0,
        tiled=True,
    )
    back_rows = partial_value.reshape(part_count, image_count, 1, model_width)
    returned = lax.all_to_all(back_rows, "exp", split_axis=0, concat_axis=2, tiled=True)
    input_grads = returned.reshape(image_count, slot_count, group_size, model_width).sum(axis=2)
    input_grads = input_grads.astype(jnp.bfloat16)
    combine_grad = jnp.einsum(
        "bmd,bsd->bms", grad_out, slot_out, preferred_element_type=jnp.float32
    )
    dispatch_grad = jnp.einsum(
        "bmd,bsd->bms", tokens, input_grads, preferred_element_type=jnp.float32
    )
    logit_grads = dispatch * (
        dispatch_grad - jnp.sum(dispatch * dispatch_grad, axis=1, keepdims=True)
    )
    logit_grads = logit_grads + combine * (
        combine_grad - jnp.sum(combine * combine_grad, axis=2, keepdims=True)
    )
    logit_grads = logit_grads.astype(jnp.bfloat16)
    token_grads = jnp.einsum("bms,ds->bmd", logit_grads, router, preferred_element_type=jnp.float32)
    token_grads = token_grads + jnp.einsum(
        "bms,bsd->bmd", dispatch_w, input_grads, preferred_element_type=jnp.float32
    )
    router_local = jnp.einsum(
        "bmd,bms->ds", tokens, logit_grads, preferred_element_type=jnp.float32
    )
    router_total = lax.psum(router_local, ("img", "exp"))
    return (token_grads.astype(jnp.bfloat16), in_gradient[None], out_gradient[None], router_total)


def solution(mesh):
    in_specs = (
        P(("img", "exp"), None, None),
        P(),
        P(("img", "exp"), None, None),
        P(("img", "exp"), None, None),
        P("img", "exp", None),
        P("exp", "img", None),
        P("exp", "img", None),
    )
    out_specs = (P(("img", "exp"), None, None), P("exp", "img", None), P("exp", "img", None), P())
    return jax.shard_map(
        on_device, mesh=mesh, in_specs=in_specs, out_specs=out_specs, check_vma=False
    )
```

profile of v0, /device:TPU:1, one launch (start us, length us, event | category | flops | bytes accessed | tf_op | source)
XLA Modules:
  0.0 600.4 jit_solution(3546550920782664651)
XLA Ops:
  7.2 0.0 copy-start
  7.2 0.0 all-gather.3.cloned.1.call-start
  7.2 0.7 all-gather.3.cloned.1.call-update
  7.9 0.8 copy-done
  8.7 1.6 fusion.56
  10.3 0.4 fusion.66
  10.7 1.9 fusion.67
  12.7 0.5 fusion.29
  13.2 1.9 fusion.30
  15.1 0.1 pad_maximum_fusion
  15.2 1.0 copy.29
  16.3 3.9 broadcast_in_dim.6
  20.2 10.5 %all-to-all-start = ((bf16[2,12,64,1280]{3,0,1,2:T(2,128)(2,1)}), bf16[2,12,64,1280]{3,0,1,2:T(2,128)(2,1)}, u32[]{:S(2)}, u32[]{:S(2)}) async-start(bf16[2,12,64,1280]{3,0,1,2:T(2,128)(2,1)} %bitcast.92), calls=%async_computation | async-start | bytes 7864320 | tf_op jit(solution)/shard_map/all_to_all | solution.py:29
  30.7 0.0 all-gather.5.cloned.1.call-start
  30.7 0.7 all-gather.5.cloned.1.call-update
  31.4 0.2 reduce-scatter.5.cloned.1.call-start
  31.7 96.4 %all-to-all-done = bf16[2,12,64,1280]{3,0,1,2:T(2,128)(2,1)} async-done(((bf16[2,12,64,1280]{3,0,1,2:T(2,128)(2,1)}), bf16[2,12,64,1280]{3,0,1,2:T(2,128)(2,1)}, u32[]{:S(2)}, u32[]{:S(2)}) %all-to-all-start) | async-done | bytes 3932192 | tf_op jit(solution)/shard_map/all_to_all | solution.py:29
  128.0 21.0 %slice_reduce_fusion = (bf16[64,12,1280]{2,1,0:T(8,128)(2,1)}, bf16[64,12,1280]{2,1,0:T(8,128)(2,1)}) fusion(bf16[2,64,12,1,1280]{4,0,2,1,3:T(2,128)(2,1)} %bitcast.5), kind=kLoop, calls=%fused_computation.31 | loop fusion | bytes 7864320 | tf_op jit(solution)/shard_map/slice | solution.py:31
  149.1 4.0 squeeze.10
  153.1 7.1 %convolution_convert_fusion = bf16[1280,1280]{1,0:T(8,128)(2,1)} fusion(bf16[768,1280]{1,0:T(8,128)(2,1)} %squeeze.10, bf16[768,1,1280]{2,0,1:T(8,128)(2,1)} %param.11), kind=kOutput, calls=%fused_computation.9 | convolution fusion | flops 2528051200 | bytes 7208960 | tf_op jit(solution)/shard_map/dot_general | solution.py:56
  160.1 0.0 reduce-scatter.5.cloned.1.call-update
  160.1 0.0 all-gather.3.cloned.1.call-done
  160.2 9.0 %fusion.11 = bf16[768,1280]{1,0:T(8,128)(2,1)} fusion(bf16[768,1,1280]{2,0,1:T(8,128)(2,1)} %param.11, bf16[768,1280]{1,0:T(8,128)(2,1)} %squeeze.10, bf16[1,1280,1280]{2,1,0:T(8,128)(2,1)} %all-gather.3.cloned.1.call-done), kind=kOutput, calls=%fused_computation.19 | convolution fusion | flops 2537226240 | bytes 9175040 | tf_op jit(solution)/shard_map/dot_general | solution.py:36
  169.2 4.0 dot_general.48
  173.2 6.5 %all-gather.5.cloned.1.call-done = bf16[1,1280,1280]{2,1,0:T(8,128)(2,1)} async-done(((bf16[1,320,1280]{2,1,0:T(8,128)(2,1)}), bf16[1,1280,1280]{2,1,0:T(8,128)(2,1)}) %all-gather.5.cloned.1.call-update) | async-done | bytes 3276816 | tf_op jit(solution)/shard_map/all_gather | solution.py:44
  179.8 5.7 convolution_bitcast_fusion
  185.5 6.0 copy.31
  191.4 8.4 %all-to-all-start.1 = ((f32[64,12,1,1280]{3,2,1,0:T(1,128)}), f32[64,12,1,1280]{3,2,1,0:T(1,128)}, u32[]{:S(2)}, u32[]{:S(2)}) async-start(f32[64,12,1,1280]{3,2,1,0:T(1,128)} %copy.31), calls=%async_computation.1 | async-start | bytes 7864320 | tf_op jit(solution)/shard_map/all_to_all | solution.py:62
  199.8 0.0 reduce-scatter.3.cloned.1.call-start
  199.9 4.0 squeeze.12
  203.9 6.6 %convolution_convert_fusion.1 = bf16[1280,1280]{1,0:T(8,128)(2,1)} fusion(bf16[768,1280]{1,0:T(8,128)(2,1)} %squeeze.12, bf16[768,1280]{1,0:T(8,128)(2,1)} %fusion.11), kind=kOutput, calls=%fused_computation.10 | convolution fusion | flops 2518220800 | bytes 7208960 | tf_op jit(solution)/shard_map/dot_general | solution.py:49
  210.5 0.0 copy-start.1
  210.5 0.0 reduce-scatter.3.cloned.1.call-update
  210.5 0.3 all-reduce.2.cloned.1.call-start
  210.9 0.7 copy-done.1
  211.5 2.2 fusion.68
  213.7 90.3 %all-to-all-done.1 = f32[64,12,1,1280]{3,2,1,0:T(1,128)} async-done(((f32[64,12,1,1280]{3,2,1,0:T(1,128)}), f32[64,12,1,1280]{3,2,1,0:T(1,128)}, u32[]{:S(2)}, u32[]{:S(2)}) %all-to-all-start.1) | async-done | bytes 3932192 | tf_op jit(solution)/shard_map/all_to_all | solution.py:62
  304.0 5.1 copy.37
  309.1 3.1 reduce_sum.47
  312.2 0.0 copy-start.2
  312.2 0.6 convolution_bitcast_fusion.2
  312.8 1.9 fusion.43
  314.7 1.1 convolution_bitcast_fusion.1
  315.8 0.0 copy-done.2
  315.8 2.7 fusion.48
  318.5 0.0 all-reduce.2.cloned.1.call-update
  318.5 4.6 fusion.23
  323.1 0.0 reduce-scatter.5.cloned.1.call-done
  323.1 23.7 %reduce-scatter.3.cloned.1.call-done = bf16[320,1280]{1,0:T(8,128)(2,1)} async-done(((bf16[1280,1280]{1,0:T(8,128)(2,1)}), bf16[320,1280]{1,0:T(8,128)(2,1)}) %reduce-scatter.3.cloned.1.call-update) | async-done | bytes 819216 | tf_op jit(solution)/shard_map/reduce_scatter | solution.py:48
  346.8 245.5 %all-reduce.2.cloned.1.call-done = f32[1280,16]{0,1:T(8,128)} async-done(((f32[1280,16]{0,1:T(8,128)}), f32[1280,16]{0,1:T(8,128)}) %all-reduce.2.cloned.1.call-update) | async-done | bytes 81936 | tf_op jit(solution)/shard_map/psum | solution.py:85
  592.3 1.5 copy.45
Async XLA Ops:
  7.2 1.6 copy-start
  7.2 153.0 %all-gather.3.cloned.1.call-start = ((), (), s32[]{:S(2)}) async-start(), calls=%async_computation.4 | async-start | bytes 4096000 | tf_op jit(solution)/shard_map/all_gather | solution.py:38
  20.2 107.9 %all-to-all-start = ((bf16[2,12,64,1280]{3,0,1,2:T(2,128)(2,1)}), bf16[2,12,64,1280]{3,0,1,2:T(2,128)(2,1)}, u32[]{:S(2)}, u32[]{:S(2)}) async-start(bf16[2,12,64,1280]{3,0,1,2:T(2,128)(2,1)} %bitcast.92), calls=%async_computation | async-start | bytes 7864320 | tf_op jit(solution)/shard_map/all_to_all | solution.py:29
  30.7 149.1 %all-gather.5.cloned.1.call-start = ((), (), s32[]{:S(2)}) async-start(), calls=%async_computation.5 | async-start | bytes 4096000 | tf_op jit(solution)/shard_map/all_gather | solution.py:44
  31.4 291.7 %reduce-scatter.5.cloned.1.call-start = ((), (), s32[]{:S(2)}) async-start(), calls=%async_computation.7 | async-start | bytes 4096000 | tf_op jit(solution)/shard_map/reduce_scatter | solution.py:55
  191.4 112.6 %all-to-all-start.1 = ((f32[64,12,1,1280]{3,2,1,0:T(1,128)}), f32[64,12,1,1280]{3,2,1,0:T(1,128)}, u32[]{:S(2)}, u32[]{:S(2)}) async-start(f32[64,12,1,1280]{3,2,1,0:T(1,128)} %copy.31), calls=%async_computation.1 | async-start | bytes 7864320 | tf_op jit(solution)/shard_map/all_to_all | solution.py:62
  199.8 147.0 %reduce-scatter.3.cloned.1.call-start = ((), (), s32[]{:S(2)}) async-start(), calls=%async_computation.6 | async-start | bytes 4096000 | tf_op jit(solution)/shard_map/reduce_scatter | solution.py:48
  210.5 1.0 copy-start.1
  210.5 381.8 %all-reduce.2.cloned.1.call-start = ((), (), s32[]{:S(2)}) async-start(), calls=%async_computation.8 | async-start | bytes 163840 | tf_op jit(solution)/shard_map/psum | solution.py:85
  312.2 3.6 copy-start.2
Sparse Core Ops, SparseCore 0:
  9.8 97.2 all-gather.2
  108.9 70.7 all-gather.4
  182.9 88.0 reduce-scatter.4
  274.0 72.8 reduce-scatter.2
  352.8 239.5 all-reduce.1
where the time goes:
time: 601 us; the launch traced here: 600 us
  waiting for transfers between devices  464 us (77%)
  local copies, waits for them, and re-layouts  52 us (9%)
  matrix products  43.7 us (7%)
  starting transfers between devices  19.6 us (3%)
  between operations  13.9 us (2%)
  other arithmetic  7.38 us (1%)
    psum x1, waiting for transfers between devices, on_device(): router_total = lax.psum(router_local, ('img', 'exp'))  245 us
    all_to_all x1, waiting for transfers between devices, on_device(): lax.all_to_all(outgoing, 'exp', split_axis=2, concat_axis=1, tiled=True)  96.4 us
    all_to_all x1, waiting for transfers between devices, on_device(): lax.all_to_all(back_rows, 'exp', split_axis=0, concat_axis=2, tiled=True)  90.3 us
    reduce_scatter x1, waiting for transfers between devices, on_device(): lax.psum_scatter(jnp.dot(columns.T, pre_grad, preferred_element_type=jnp....  23.7 us
    slice x1, local copies, waits for them, and re-layouts, on_device(): expert_inputs = rows_in[0]  21 us
  transfers between devices with their start and end apart: 7, of which 5 were waited for; matrix products, arithmetic and copies ran while one was open for 17% of the time, Pallas kernels for 0%

commit v1 on v0

v1 whole, which is shorter than its diff:
```python
import functools

import jax
import jax.numpy as jnp
from jax import lax
from jax.experimental import pallas as pl
from jax.experimental.pallas import tpu as pltpu
from jax.sharding import Mesh, PartitionSpec as P

BF16 = jnp.bfloat16
F32 = jnp.float32
IMG = ("zh1", "zh0")
EXP = ("x", "zl", "yh", "yl", "c")
AXES = IMG + EXP
EXPERT = ("x", "zl", "yh")
PAD = 16
VMEM_LIMIT = 48 * 1024 * 1024


def gelu_tanh(values):
    return jax.nn.gelu(values, approximate=True)


def dot(a, b, dims):
    return lax.dot_general(a, b, (dims, ((), ())), preferred_element_type=F32)


NN = ((1,), (0,))
NT = ((1,), (1,))
TN = ((0,), (0,))


def own_image(rows, columns, token_count):
    image = lax.broadcasted_iota(jnp.int32, (rows, columns), 0) // token_count
    return image == lax.broadcasted_iota(jnp.int32, (rows, columns), 1) % PAD


def front_kernel(token_count, tokens, grad_out, router, grads_out, inputs_out, dispatch_out, combine_out):
    rows = tokens.shape[0]
    columns = router.shape[1]
    images = rows // token_count
    logits = dot(tokens[...], router[...], NN)
    mine = own_image(rows, columns, token_count)
    weights = jnp.exp(logits - jnp.max(logits, axis=1, keepdims=True))
    weights = jnp.where(mine, weights, 0.0)
    combine = weights / jnp.sum(weights, axis=1, keepdims=True)
    grads_out[...] = dot(combine.astype(BF16), grad_out[...], TN).astype(BF16)
    combine_out[...] = combine
    by_image = logits.reshape(images, token_count, columns)
    weights = jnp.exp(by_image - jnp.max(by_image, axis=1, keepdims=True))
    dispatch = weights / jnp.sum(weights, axis=1, keepdims=True)
    dispatch = jnp.where(mine, dispatch.reshape(rows, columns), 0.0)
    inputs_out[...] = dot(dispatch.astype(BF16), tokens[...], TN).astype(BF16)
    dispatch_out[...] = dispatch


def combine_kernel(slot_count, grad_out, slot_out, combine, term_out):
    count = slot_out.shape[0]
    columns = combine.shape[1]
    row = lax.broadcasted_iota(jnp.int32, (columns, count), 0)
    source = lax.broadcasted_iota(jnp.int32, (columns, count), 1)
    order = (source == (row % PAD) * slot_count + row // PAD).astype(BF16)
    outputs = dot(order, slot_out[...], NN).astype(BF16)
    weights = combine[...]
    grads = weights * dot(grad_out[...], outputs, NT)
    term_out[...] = grads - weights * jnp.sum(grads, axis=1, keepdims=True)


def logit_kernel(token_count, slot_count, tokens, dispatch, term, input_grads, logit_out, router_out):
    rows, columns = dispatch.shape
    images = rows // token_count
    weights = dispatch[...]
    grads = weights * dot(tokens[...], input_grads[...], NT)
    total = jnp.sum(grads.reshape(images, token_count, columns), axis=1, keepdims=True)
    total = jnp.broadcast_to(total, (images, token_count, columns)).reshape(rows, columns)
    logit_grads = (grads - weights * total + term[...]).astype(BF16)
    logit_out[...] = logit_grads
    column = lax.broadcasted_iota(jnp.int32, (columns, slot_count), 0) // PAD
    fold = (column == lax.broadcasted_iota(jnp.int32, (columns, slot_count), 1)).astype(BF16)
    by_slot = dot(logit_grads, fold, NN).astype(BF16)
    router_out[...] = dot(by_slot, tokens[...], TN)


def token_kernel(dispatch, logit_grads, router, input_grads, tokens_out):
    total = dot(logit_grads[...], router[...], NT)
    total = total + dot(dispatch[...].astype(BF16), input_grads[...], NN)
    tokens_out[...] = total.astype(BF16)


def local_call(kernel, outs, *operands):
    whole = pl.BlockSpec(memory_space=pltpu.VMEM)
    return pl.pallas_call(
        kernel,
        out_shape=[jax.ShapeDtypeStruct(shape, dtype) for shape, dtype in outs],
        in_specs=[whole] * len(operands),
        out_specs=[whole] * len(outs),
        compiler_params=pltpu.CompilerParams(vmem_limit_bytes=VMEM_LIMIT),
    )(*operands)


def swap(values, axis, mask):
    count = lax.axis_size(axis)
    return lax.ppermute(values, axis, [(k, k ^ mask) for k in range(count)])


def to_image_pair(values):
    return swap(values, IMG, 3)


def to_weight_pair(values):
    return swap(values, IMG, 1)


def flip_blocks(blocks):
    zh1, zh0 = lax.axis_index("zh1"), lax.axis_index("zh0")
    blocks = [jnp.where(zh0 == 0, blocks[k], blocks[k ^ 1]) for k in range(4)]
    return [jnp.where(zh1 == 0, blocks[k], blocks[k ^ 2]) for k in range(4)]


def sum_everywhere(values):
    for axes in (("yl", "c"), ("x",), ("zl", "yh"), IMG):
        first, second, third = (swap(values, axes, mask) for mask in (1, 2, 3))
        values = (values + first) + (second + third)
    return values


def share(values):
    values = jnp.concatenate([values, swap(values, "yl", 1)])
    return jnp.concatenate([values, swap(values, "c", 1)])


def gather_share(values):
    half = values.shape[0] // 2
    values = values[:half] + swap(values[half:].astype(BF16), "c", 1).astype(F32)
    half = half // 2
    return values[:half] + swap(values[half:].astype(BF16), "yl", 1).astype(F32)


def on_device(tokens, router, grad_out, slot_out, hidden_pre, w_in, w_out):
    image_count, token_count, model_width = tokens.shape
    slot_count = router.shape[1]
    rows = image_count * token_count
    columns = slot_count * PAD
    group = slot_count * image_count
    zh1, zh0 = lax.axis_index("zh1"), lax.axis_index("zh0")
    yl, c = lax.axis_index("yl"), lax.axis_index("c")
    first_half = zh1 == 0

    hidden_pre = hidden_pre.reshape(-1, hidden_pre.shape[2])
    part = hidden_pre.shape[1] // 2
    pre_mine = jnp.where(first_half, hidden_pre[:, :part], hidden_pre[:, part:])
    pre_other = to_image_pair(jnp.where(first_half, hidden_pre[:, part:], hidden_pre[:, :part]))
    w_in, w_out = w_in[0], w_out[0]
    share_rows = w_in.shape[0]
    w_in_mine = jnp.where(first_half, w_in[:, :part], w_in[:, part:])
    w_in_pair = to_image_pair(jnp.where(first_half, w_in[:, part:], w_in[:, :part]))
    w_out_pair = to_weight_pair(w_out)

    tokens = tokens.reshape(rows, model_width)
    grad_out = grad_out.reshape(rows, model_width)
    router_wide = jnp.repeat(router, PAD, axis=1)
    slots = ((columns, model_width), BF16)
    wide = ((rows, columns), F32)
    slot_grads, slot_inputs, dispatch, combine = local_call(
        functools.partial(front_kernel, token_count),
        [slots, slots, wide, wide],
        tokens, grad_out, router_wide,
    )
    padded = lax.broadcasted_iota(jnp.int32, (group, columns), 1)
    row = lax.broadcasted_iota(jnp.int32, (group, columns), 0)
    pick = (padded == row // image_count * PAD + row % image_count).astype(BF16)

    def to_experts(values):
        values = lax.all_to_all(values, EXPERT, 0, 0, tiled=True)
        return dot(pick, values, NN).astype(BF16)

    slot_grads = to_experts(slot_grads)
    slot_grads_other = to_image_pair(slot_grads)
    slot_inputs = to_experts(slot_inputs)
    slot_inputs_other = to_image_pair(slot_inputs)
    grads_mine, grads_other = share(slot_grads), share(slot_grads_other)
    inputs_mine, inputs_other = share(slot_inputs), share(slot_inputs_other)

    (term,) = local_call(
        functools.partial(combine_kernel, slot_count), [wide],
        grad_out, slot_out.reshape(-1, model_width), combine,
    )

    count = hidden_pre.shape[0]
    place = lax.broadcasted_iota(jnp.int32, (count, count), 0)
    source = lax.broadcasted_iota(jnp.int32, (count, count), 1)
    member_c = (place // (2 * group)) ^ c
    member_y = (place // group % 2) ^ yl
    wanted = (place % group // image_count * 4 + member_y * 2 + member_c) * image_count + place % image_count
    order = (source == wanted).astype(BF16)
    pre_mine = dot(order, pre_mine, NN)
    pre_other = dot(order, pre_other, NN)

    w_out_half = jnp.where(
        zh0 == 0, jnp.concatenate([w_out, w_out_pair]), jnp.concatenate([w_out_pair, w_out])
    )
    w_in_both = to_weight_pair(jnp.concatenate([w_in_mine, w_in_pair]))
    w_in_half = jnp.concatenate(
        flip_blocks([w_in_mine, w_in_both[:share_rows], w_in_both[share_rows:], w_in_pair])
    )

    def expert(pre_values, grads):
        activation, gelu_back = jax.vjp(gelu_tanh, pre_values)
        hidden_grad = dot(grads, w_out_half, NT)
        pre_grad = gelu_back(hidden_grad)[0].astype(BF16)
        return activation.astype(BF16), pre_grad

    act_other, pre_grad_other = expert(pre_other, grads_other)
    act_mine, pre_grad_mine = expert(pre_mine, grads_mine)
    back_other = gather_share(dot(pre_grad_other, w_in_half, NT))
    back_other = to_image_pair(back_other.astype(BF16))
    back_mine = gather_share(dot(pre_grad_mine, w_in_half, NT))
    back = (back_mine + back_other.astype(F32)).astype(BF16)
    back = dot(pick, back, TN).astype(BF16)
    input_grads = lax.all_to_all(back, EXPERT, 0, 0, tiled=True)

    logit_grads, router_grads = local_call(
        functools.partial(logit_kernel, token_count, slot_count),
        [((rows, columns), BF16), ((slot_count, model_width), F32)],
        tokens, dispatch, term, input_grads,
    )
    router_total = sum_everywhere(router_grads)
    (token_grads,) = local_call(
        token_kernel, [((rows, model_width), BF16)],
        dispatch, logit_grads, router_wide, input_grads,
    )

    out_partial = dot(act_other, grads_other, TN) + dot(act_mine, grads_mine, TN)
    out_first, out_second = out_partial[:share_rows], out_partial[share_rows:]
    out_sent = jnp.where(zh0 == 0, out_second, out_first).astype(BF16)
    out_gradient = jnp.where(zh0 == 0, out_first, out_second)
    out_gradient = (out_gradient + to_weight_pair(out_sent).astype(F32)).astype(BF16)

    in_partial = dot(inputs_other, pre_grad_other, TN) + dot(inputs_mine, pre_grad_mine, TN)
    blocks = flip_blocks([in_partial[k * share_rows:(k + 1) * share_rows] for k in range(4)])
    in_arrived = to_weight_pair(jnp.concatenate([blocks[1], blocks[2]]).astype(BF16)).astype(F32)
    in_mine = (blocks[0] + in_arrived[:share_rows]).astype(BF16)
    in_pair = to_image_pair((blocks[3] + in_arrived[share_rows:]).astype(BF16))
    in_gradient = jnp.where(
        first_half,
        jnp.concatenate([in_mine, in_pair], axis=1),
        jnp.concatenate([in_pair, in_mine], axis=1),
    )
    return (
        token_grads.reshape(image_count, token_count, model_width),
        in_gradient[None],
        out_gradient[None],
        router_total.T,
    )


def solution(mesh):
    fine = Mesh(mesh.devices.reshape(2, 2, 4, 2, 2, 2, 2), AXES)
    in_specs = (
        P(AXES, None, None),
        P(),
        P(AXES, None, None),
        P(AXES, None, None),
        P(IMG, EXP, None),
        P(EXP, IMG, None),
        P(EXP, IMG, None),
    )
    out_specs = (P(AXES, None, None), P(EXP, IMG, None), P(EXP, IMG, None), P())
    return jax.shard_map(
        on_device, mesh=fine, in_specs=in_specs, out_specs=out_specs, check_vma=False
    )
```

time: 601 us -> 351 us (0.58)
  waiting for transfers between devices: 464 us -> 175 us
  starting transfers between devices: 19.6 us -> 90.9 us
  local copies, waits for them, and re-layouts: 52 us -> 10.7 us
  between operations: 13.9 us -> 1.65 us
  Pallas kernels: 0 us -> 9.9 us
  other arithmetic: 7.38 us -> 15.4 us
    psum x1 -> x0, waiting for transfers between devices: 245 us -> none  [on_device(): router_total = lax.psum(router_local, ('img', 'exp'))]
    all_to_all x2 -> x3, waiting for transfers between devices: 187 us -> 0.01 us  [the longest x2 0.01 us: to_experts(): values = lax.all_to_all(values, EXPERT, 0, 0, tiled=True)]
    ppermute x0 -> x34, waiting for transfers between devices: none -> 175 us  [swap(): return lax.ppermute(values, axis, [(k, k ^ mask) for k in range(count)])]
    ppermute x0 -> x34, starting transfers between devices: none -> 64 us  [swap(): return lax.ppermute(values, axis, [(k, k ^ mask) for k in range(count)])]
    reduce_scatter x2 -> x0, waiting for transfers between devices: 23.7 us -> none  [the longest x1 23.7 us: on_device(): lax.psum_scatter(jnp.dot(columns.T, pre_grad, preferred_element_type=jnp....]
    slice x1 -> x4, local copies, waits for them, and re-layouts: 21 us -> 0.3 us  [the longest x2 0.2 us: gather_share(): values[half:].astype(BF16)]
    dot_general x2 -> x0, local copies, waits for them, and re-layouts: 9.97 us -> none  [on_device(): jnp.dot(pre_grad, lax.all_gather(w_in, 'img', axis=1, tiled=True)[0].T, p...]
    pallas_call x0 -> x4, Pallas kernels: none -> 9.9 us  [local_call(): pl.pallas_call(kernel, out_shape=[jax.ShapeDtypeStruct(shape, dtype) for...]
  transfers between devices with their start and end apart: 7 -> 37, of which waited for: 5 -> 14; matrix products, arithmetic and copies ran while one was open for 17% -> 17% of each run, Pallas kernels for 0% -> 2%
where the time goes in v1:
time: 351 us; the launch traced here: 346 us
  waiting for transfers between devices  175 us (50%)
  starting transfers between devices  90.9 us (26%)
  matrix products  42.5 us (12%)
  other arithmetic  15.4 us (4%)
  local copies, waits for them, and re-layouts  10.7 us (3%)
  Pallas kernels  9.9 us (3%)
    ppermute x34, waiting for transfers between devices, swap(): return lax.ppermute(values, axis, [(k, k ^ mask) for k in range(count)])  175 us
    ppermute x34, starting transfers between devices, swap(): return lax.ppermute(values, axis, [(k, k ^ mask) for k in range(count)])  64 us
    dot_general x13, matrix products, dot(): return lax.dot_general(a, b, (dims, ((), ())), preferred_element_type=F32)  42.5 us
    all_to_all x2, starting transfers between devices, to_experts(): values = lax.all_to_all(values, EXPERT, 0, 0, tiled=True)  16.6 us
    all_to_all x1, starting transfers between devices, on_device(): input_grads = lax.all_to_all(back, EXPERT, 0, 0, tiled=True)  10.3 us
    pallas_call x4, Pallas kernels, local_call(): pl.pallas_call(kernel, out_shape=[jax.ShapeDtypeStruct(shape, dtype) for...  9.9 us
    unnamed x90, local copies, waits for them, and re-layouts  9.16 us
  transfers between devices with their start and end apart: 37, of which 14 were waited for; matrix products, arithmetic and copies ran while one was open for 17% of the time, Pallas kernels for 2%

profile of v1, /device:TPU:1, one launch (start us, length us, event | category | flops | bytes accessed | tf_op | source)
XLA Modules:
  0.0 345.8 jit_solution(12172951983299195533)
XLA Ops:
  2.2 4.4 %shard_map.102 = (bf16[256,1280]{1,0:T(8,128)(2,1)S(1)}, bf16[256,1280]{1,0:T(8,128)(2,1)S(1)}, f32[768,256]{1,0:T(8,128)S(1)}, f32[768,256]{1,0:T(8,128)S(1)}) custom-call(bf16[768,1280]{1,0:T(8,128)(2,1)S(1)} %bitcast.32, bf16[768,1280]{1,0:T(8,128)(2,1)} %bitcast.30, bf16[1280,256]{1,0:T(8,128)(2,1)S(1)} %copy.12.router), custom_call_target="tpu_custom_call" | custom-call | tf_op jit(solution)/shard_map/pallas_call | solution.py:92
  9.2 9.1 %all-to-all-start = ((bf16[16,16,1280]{2,1,0:T(8,128)(2,1)}), bf16[16,16,1280]{2,1,0:T(8,128)(2,1)}, u32[]{:S(2)}, u32[]{:S(2)}) async-start(bf16[16,16,1280]{2,1,0:T(8,128)(2,1)} %bitcast.37), calls=%async_computation | async-start | bytes 1310720 | tf_op jit(solution)/shard_map/all_to_all | solution.py:174
  18.3 2.6 broadcast_select_fusion
  20.9 5.1 %collective-permute-start.10 = (bf16[768,640]{1,0:T(8,128)(2,1)}, bf16[768,640]{1,0:T(8,128)(2,1)}, u32[]{:S(2)}, u32[]{:S(2)}) collective-permute-start(bf16[768,640]{1,0:T(8,128)(2,1)} %broadcast_select_fusion), channel_id=1, source_target_pairs={{0,192},{64,128},{128,64},{192,0},{1,193},{65,129},{129,65},{193,1... | collective-permute-start | bytes 2949128 | tf_op jit(solution)/shard_map/ppermute | solution.py:103
  26.0 1.2 collective-permute-start.2
  28.6 5.1 %fusion.49 = f32[768,640]{1,0:T(8,128)} fusion(pred[]{:T(512)S(6)} %eq.21, bf16[768,1280]{1,0:T(8,128)(2,1)} %bitcast.42, s32[768]{0:T(1024)S(1)} %get-tuple-element.30, s32[768]{0:T(1024)S(1)} %get-tuple-element.31, s32[]{:T(128)S(6)} %axis_index.64, s32[768]{0:T(1024)S(1)} %get-tuple-element.26, s32[768]{0:T(1024)S(1)} %get-tuple-element.36, ...), kind=kOutput, calls=%fused_computation.86 | convolution fusion | flops 774340608 | bytes 3959817 | tf_op jit(solution)/shard_map/dot_general | solution.py:25
  34.8 1.2 shard_map.103.term
  36.9 7.5 %all-to-all-start.2 = ((bf16[16,16,1280]{2,1,0:T(8,128)(2,1)}), bf16[16,16,1280]{2,1,0:T(8,128)(2,1)S(1)}, u32[]{:S(2)}, u32[]{:S(2)}) async-start(bf16[16,16,1280]{2,1,0:T(8,128)(2,1)} %bitcast.36), calls=%async_computation.2 | async-start | bytes 1310720 | tf_op jit(solution)/shard_map/all_to_all | solution.py:174
  44.5 40.8 %collective-permute-done.3 = bf16[320,640]{1,0:T(8,128)(2,1)} collective-permute-done((bf16[320,640]{1,0:T(8,128)(2,1)}, bf16[320,640]{1,0:T(8,128)(2,1)}, u32[]{:S(2)}, u32[]{:S(2)}) %collective-permute-start.3) | collective-permute-done | bytes 409632 | tf_op jit(solution)/shard_map/ppermute | solution.py:103
  85.3 2.1 pad_maximum_fusion.6
  87.4 1.9 collective-permute-start.4
  89.3 1.5 convolution_convert_fusion.2
  90.9 2.5 collective-permute-start.7
  93.5 5.0 %fusion.92 = f32[768,640]{1,0:T(8,128)} fusion(bf16[768,640]{1,0:T(8,128)(2,1)} %collective-permute-done.10, s32[768]{0:T(1024)S(1)} %copy-done.20, s32[768]{0:T(1024)S(1)} %copy-done.22, s32[]{:T(128)S(6)} %axis_index.64, s32[768]{0:T(1024)S(1)} %get-tuple-element.26, s32[768]{0:T(1024)S(1)} %copy-done.28, s32[]{:T(128)S(6)} %axis_index.30, ...), kind=kOutput, calls=%fused_computation.172 | convolution fusion | flops 773849088 | bytes 2976776 | tf_op jit(solution)/shard_map/dot_general | solution.py:25
  99.3 1.4 collective-permute-start.17
  100.7 24.1 %collective-permute-done.4 = bf16[640,640]{1,0:T(8,128)(2,1)S(1)} collective-permute-done((bf16[640,640]{1,0:T(8,128)(2,1)}, bf16[640,640]{1,0:T(8,128)(2,1)S(1)}, u32[]{:S(2)}, u32[]{:S(2)}) %collective-permute-start.4) | collective-permute-done | bytes 819232 | tf_op jit(solution)/shard_map/ppermute | solution.py:103
  124.9 1.1 collective-permute-start.14
  126.4 1.2 broadcast_select_fusion.8
  127.6 1.1 pad_maximum_fusion.2
  128.7 2.9 collective-permute-start.1
  131.6 13.2 %collective-permute-done.14 = bf16[192,1280]{1,0:T(8,128)(2,1)S(1)} collective-permute-done((bf16[192,1280]{1,0:T(8,128)(2,1)S(1)}, bf16[192,1280]{1,0:T(8,128)(2,1)S(1)}, u32[]{:S(2)}, u32[]{:S(2)}) %collective-permute-start.14) | collective-permute-done | bytes 491552 | tf_op jit(solution)/shard_map/ppermute | solution.py:103
  145.3 3.5 %collective-permute-start.9 = (bf16[384,1280]{1,0:T(8,128)(2,1)S(1)}, bf16[384,1280]{1,0:T(8,128)(2,1)S(1)}, u32[]{:S(2)}, u32[]{:S(2)}) collective-permute-start(bf16[384,1280]{1,0:T(8,128)(2,1)S(1)} %pad_maximum_fusion.3), channel_id=1, source_target_pairs={{0,1},{1,0},{2,3},{3,2},{4,5},{5,4},{6,7},{7,6},{8,9},{9,8},{10,11... | collective-permute-start | bytes 2949128 | tf_op jit(solution)/shard_map/ppermute | solution.py:103
  149.0 5.4 %collective-permute-done.15 = bf16[192,1280]{1,0:T(8,128)(2,1)S(1)} collective-permute-done((bf16[192,1280]{1,0:T(8,128)(2,1)S(1)}, bf16[192,1280]{1,0:T(8,128)(2,1)S(1)}, u32[]{:S(2)}, u32[]{:S(2)}) %collective-permute-start.15) | collective-permute-done | bytes 491552 | tf_op jit(solution)/shard_map/ppermute | solution.py:103
  155.4 4.1 %collective-permute-start.16 = (bf16[384,1280]{1,0:T(8,128)(2,1)}, bf16[384,1280]{1,0:T(8,128)(2,1)}, u32[]{:S(2)}, u32[]{:S(2)}) collective-permute-start(bf16[384,1280]{1,0:T(8,128)(2,1)} %pad_maximum_fusion.4), channel_id=1, source_target_pairs={{0,1},{1,0},{2,3},{3,2},{4,5},{5,4},{6,7},{7,6},{8,9},{9,8},{10,11... | collective-permute-start | bytes 2949128 | tf_op jit(solution)/shard_map/ppermute | solution.py:103
  159.7 5.2 %fusion.25 = bf16[768,640]{1,0:T(8,128)(2,1)S(1)} fusion(f32[768,640]{1,0:T(8,128)S(1)} %copy-done.40, bf16[768,1280]{1,0:T(8,128)(2,1)S(1)} %constant_dynamic-update-slice_fusion, bf16[320,1280]{1,0:T(8,128)(2,1)} %collective-permute-done.2, bf16[320,1280]{1,0:T(8,128)(2,1)} %bitcast.6, pred[]{:T(512)S(6)} %eq.19), kind=kOutput, calls=%fused_computation.43 | convolution fusion | flops 1275494400 | bytes 6553601 | tf_op jit(solution)/shard_map/dot_general | solution.py:25
  165.9 1.7 fusion.60
  167.8 4.8 %fusion.18 = bf16[768,640]{1,0:T(8,128)(2,1)S(1)} fusion(f32[768,640]{1,0:T(8,128)S(1)} %copy-done.43, bf16[384,1280]{1,0:T(8,128)(2,1)S(1)} %collective-permute-done.1, bf16[192,1280]{1,0:T(8,128)(2,1)} %collective-permute-done, bf16[192,1280]{1,0:T(8,128)(2,1)S(1)} %convolution_convert_fusion.2, bf16[320,1280]{1,0:T(8,128)(2,1)} %collective-permute-done.2, ...), kind=kOutput, calls=%fused_computation.36 | convolution fusion | flops 1281392640 | bytes 6553601 | tf_op jit(solution)/shard_map/dot_general | solution.py:25
  172.7 1.7 fusion.61
  174.5 9.4 %collective-permute-start.5 = (bf16[384,1280]{1,0:T(8,128)(2,1)S(1)}, bf16[384,1280]{1,0:T(8,128)(2,1)S(1)}, u32[]{:S(2)}, u32[]{:S(2)}) collective-permute-start(bf16[384,1280]{1,0:T(8,128)(2,1)S(1)} %slice.224), channel_id=1, source_target_pairs={{0,1},{1,0},{2,3},{3,2},{4,5},{5,4},{6,7},{7,6},{8,9},{9,8},{10,11... | collective-permute-start | bytes 2949128 | tf_op jit(solution)/shard_map/ppermute | solution.py:103
  184.0 3.4 fusion.31
  188.3 1.2 collective-permute-start.6
  189.5 11.0 %collective-permute-done.12 = bf16[192,1280]{1,0:T(8,128)(2,1)S(1)} collective-permute-done((bf16[192,1280]{1,0:T(8,128)(2,1)S(1)}, bf16[192,1280]{1,0:T(8,128)(2,1)S(1)}, u32[]{:S(2)}, u32[]{:S(2)}) %collective-permute-start.12) | collective-permute-done | bytes 491552 | tf_op jit(solution)/shard_map/ppermute | solution.py:103
  200.6 4.3 %collective-permute-start.13 = (bf16[192,1280]{1,0:T(8,128)(2,1)S(1)}, bf16[192,1280]{1,0:T(8,128)(2,1)S(1)}, u32[]{:S(2)}, u32[]{:S(2)}) collective-permute-start(bf16[192,1280]{1,0:T(8,128)(2,1)S(1)} %fusion.38), channel_id=1, source_target_pairs={{0,192},{64,128},{128,64},{192,0},{1,193},{65,129},{129,65},{193,1... | collective-permute-start | bytes 1474568 | tf_op jit(solution)/shard_map/ppermute | solution.py:103
  205.0 4.2 %fusion.37 = f32[640,1280]{1,0:T(8,128)} fusion(f32[768,640]{1,0:T(8,128)S(1)} %copy-done.43, bf16[384,1280]{1,0:T(8,128)(2,1)S(1)} %collective-permute-done.1, bf16[192,1280]{1,0:T(8,128)(2,1)} %collective-permute-done, bf16[192,1280]{1,0:T(8,128)(2,1)S(1)} %convolution_convert_fusion.2), kind=kOutput, calls=%fused_computation.66 | convolution fusion | flops 1268613120 | bytes 7208960 | tf_op jit(solution)/shard_map/dot_general | solution.py:25
  209.2 1.8 collective-permute-done.6
  211.1 13.7 %collective-permute-done.13 = bf16[192,1280]{1,0:T(8,128)(2,1)S(1)} collective-permute-done((bf16[192,1280]{1,0:T(8,128)(2,1)S(1)}, bf16[192,1280]{1,0:T(8,128)(2,1)S(1)}, u32[]{:S(2)}, u32[]{:S(2)}) %collective-permute-start.13) | collective-permute-done | bytes 491552 | tf_op jit(solution)/shard_map/ppermute | solution.py:103
  224.8 1.4 convolution_convert_fusion
  226.2 10.3 %all-to-all-start.1 = ((bf16[16,16,1280]{2,1,0:T(8,128)(2,1)}), bf16[16,16,1280]{2,1,0:T(8,128)(2,1)S(1)}, u32[]{:S(2)}, u32[]{:S(2)}) async-start(bf16[16,16,1280]{2,1,0:T(8,128)(2,1)} %bitcast.9), calls=%async_computation.1 | async-start | bytes 1310720 | tf_op jit(solution)/shard_map/all_to_all | solution.py:220
  236.6 4.5 %convolution_add_fusion.1 = f32[1280,640]{1,0:T(8,128)S(1)} fusion(f32[1280,640]{1,0:T(8,128)} %fusion.31, bf16[768,640]{1,0:T(8,128)(2,1)} %copy-done.42, bf16[384,1280]{1,0:T(8,128)(2,1)} %collective-permute-done.16, bf16[192,1280]{1,0:T(8,128)(2,1)S(1)} %collective-permute-done.15, bf16[192,1280]{1,0:T(8,128)(2,1)S(1)} %copy-done.16), kind=kOutput, calls=%fused_computation.7 | convolution fusion | flops 1265008640 | bytes 9502720 | tf_op jit(solution)/shard_map/dot_general | solution.py:25
  243.1 1.9 collective-permute-start.19
  245.0 3.3 convolution_add_fusion
  248.4 1.1 copy-done.4
  249.5 1.1 copy-done.6
  250.6 1.9 shard_map.104
  252.5 3.1 collective-permute-start.22
  256.1 1.3 collective-permute-start.24
  257.5 1.7 collective-permute-start.21
  259.2 39.3 %collective-permute-done.19 = bf16[640,640]{1,0:T(8,128)(2,1)} collective-permute-done((bf16[640,640]{1,0:T(8,128)(2,1)}, bf16[640,640]{1,0:T(8,128)(2,1)}, u32[]{:S(2)}, u32[]{:S(2)}) %collective-permute-start.19) | collective-permute-done | bytes 819232 | tf_op jit(solution)/shard_map/ppermute | solution.py:103
  298.5 1.3 convert_element_type.79
  299.8 1.6 collective-permute-start.25
  301.4 2.4 collective-permute-start.26
  304.4 2.1 collective-permute-done.26
  306.5 1.9 collective-permute-done.27
  308.5 2.8 collective-permute-start.28
  311.3 1.9 collective-permute-start.29
  313.2 2.8 collective-permute-done.21
  316.0 1.1 fusion.54
  317.1 10.5 %collective-permute-done.29 = f32[16,1280]{1,0:T(8,128)S(1)} collective-permute-done((f32[16,1280]{1,0:T(8,128)S(1)}, f32[16,1280]{1,0:T(8,128)S(1)}, u32[]{:S(2)}, u32[]{:S(2)}) %collective-permute-start.29) | collective-permute-done | bytes 81952 | tf_op jit(solution)/shard_map/ppermute | solution.py:103
  327.6 4.3 %collective-permute-done.30 = f32[16,1280]{1,0:T(8,128)S(1)} collective-permute-done((f32[16,1280]{1,0:T(8,128)S(1)}, f32[16,1280]{1,0:T(8,128)S(1)}, u32[]{:S(2)}, u32[]{:S(2)}) %collective-permute-start.30) | collective-permute-done | bytes 81952 | tf_op jit(solution)/shard_map/ppermute | solution.py:103
  332.1 3.0 collective-permute-start.32
  335.1 2.6 collective-permute-start.33
  337.7 1.1 maximum_select_fusion.1
  338.8 2.5 shard_map.105
  341.3 3.7 %collective-permute-done.33 = f32[16,1280]{1,0:T(8,128)S(1)} collective-permute-done((f32[16,1280]{1,0:T(8,128)S(1)}, f32[16,1280]{1,0:T(8,128)S(1)}, u32[]{:S(2)}, u32[]{:S(2)}) %collective-permute-start.33) | collective-permute-done | bytes 81952 | tf_op jit(solution)/shard_map/ppermute | solution.py:103
  (155 shorter events, 16.9 us)
Async XLA Ops:
  9.2 18.0 %copy-start.14 = (bf16[1,320,1280]{2,1,0:T(8,128)(2,1)S(1)}, bf16[1,320,1280]{2,1,0:T(8,128)(2,1)}, u32[]{:S(2)}) copy-start(bf16[1,320,1280]{2,1,0:T(8,128)(2,1)} %param.12) | copy-start | bytes 2457604
  9.2 27.7 %all-to-all-start = ((bf16[16,16,1280]{2,1,0:T(8,128)(2,1)}), bf16[16,16,1280]{2,1,0:T(8,128)(2,1)}, u32[]{:S(2)}, u32[]{:S(2)}) async-start(bf16[16,16,1280]{2,1,0:T(8,128)(2,1)} %bitcast.37), calls=%async_computation | async-start | bytes 1310720 | tf_op jit(solution)/shard_map/all_to_all | solution.py:174
  20.9 72.5 %collective-permute-start.10 = (bf16[768,640]{1,0:T(8,128)(2,1)}, bf16[768,640]{1,0:T(8,128)(2,1)}, u32[]{:S(2)}, u32[]{:S(2)}) collective-permute-start(bf16[768,640]{1,0:T(8,128)(2,1)} %broadcast_select_fusion), channel_id=1, source_target_pairs={{0,192},{64,128},{128,64},{192,0},{1,193},{65,129},{129,65},{193,1... | collective-permute-start | bytes 2949128 | tf_op jit(solution)/shard_map/ppermute | solution.py:103
  26.0 133.7 %collective-permute-start.2 = (bf16[320,1280]{1,0:T(8,128)(2,1)}, bf16[320,1280]{1,0:T(8,128)(2,1)}, u32[]{:S(2)}, u32[]{:S(2)}) collective-permute-start(bf16[320,1280]{1,0:T(8,128)(2,1)} %bitcast.6), channel_id=1, source_target_pairs={{0,64},{64,0},{128,192},{192,128},{1,65},{65,1},{129,193},{193,129... | collective-permute-start | bytes 2457608 | tf_op jit(solution)/shard_map/ppermute | solution.py:103
  28.2 57.2 %collective-permute-start.3 = (bf16[320,640]{1,0:T(8,128)(2,1)}, bf16[320,640]{1,0:T(8,128)(2,1)}, u32[]{:S(2)}, u32[]{:S(2)}) collective-permute-start(bf16[320,640]{1,0:T(8,128)(2,1)} %get-tuple-element.24), channel_id=1, source_target_pairs={{0,192},{64,128},{128,64},{192,0},{1,193},{65,129},{129,65},{193,1... | collective-permute-start | bytes 1228808 | tf_op jit(solution)/shard_map/ppermute | solution.py:103
  28.4 5.2 %copy-start.19 = (s32[768]{0:T(1024)}, s32[768]{0:T(1024)S(1)}, u32[]{:S(2)}) copy-start(s32[768]{0:T(1024)S(1)} %get-tuple-element.30) | copy-start | bytes 9220
  28.4 5.2 %copy-start.21 = (s32[768]{0:T(1024)}, s32[768]{0:T(1024)S(1)}, u32[]{:S(2)}) copy-start(s32[768]{0:T(1024)S(1)} %get-tuple-element.31) | copy-start | bytes 9220
  28.5 5.2 %copy-start.23 = (s32[768]{0:T(1024)}, s32[768]{0:T(1024)S(1)}, u32[]{:S(2)}) copy-start(s32[768]{0:T(1024)S(1)} %get-tuple-element.32) | copy-start | bytes 9220
  28.5 5.2 %copy-start.25 = (s32[768]{0:T(1024)}, s32[768]{0:T(1024)S(1)}, u32[]{:S(2)}) copy-start(s32[768]{0:T(1024)S(1)} %get-tuple-element.33) | copy-start | bytes 9220
  28.5 5.2 %copy-start.27 = (s32[768]{0:T(1024)}, s32[768]{0:T(1024)S(1)}, u32[]{:S(2)}) copy-start(s32[768]{0:T(1024)S(1)} %get-tuple-element.36) | copy-start | bytes 9220
  28.5 5.2 %copy-start.29 = (s32[768]{0:T(1024)}, s32[768]{0:T(1024)S(1)}, u32[]{:S(2)}) copy-start(s32[768]{0:T(1024)S(1)} %get-tuple-element.37) | copy-start | bytes 9220
  28.5 5.2 %copy-start.31 = (pred[768]{0:T(1024)(128)(4,1)}, pred[768]{0:T(1024)(128)(4,1)S(1)}, u32[]{:S(2)}) copy-start(pred[768]{0:T(1024)(128)(4,1)S(1)} %get-tuple-element.28) | copy-start | bytes 2308
  36.9 62.0 %all-to-all-start.2 = ((bf16[16,16,1280]{2,1,0:T(8,128)(2,1)}), bf16[16,16,1280]{2,1,0:T(8,128)(2,1)S(1)}, u32[]{:S(2)}, u32[]{:S(2)}) async-start(bf16[16,16,1280]{2,1,0:T(8,128)(2,1)} %bitcast.36), calls=%async_computation.2 | async-start | bytes 1310720 | tf_op jit(solution)/shard_map/all_to_all | solution.py:174
  44.4 48.9 %copy-start.20 = (s32[768]{0:T(1024)S(1)}, s32[768]{0:T(1024)}, u32[]{:S(2)}) copy-start(s32[768]{0:T(1024)} %copy-done.19) | copy-start | bytes 9220
  44.5 48.9 %copy-start.22 = (s32[768]{0:T(1024)S(1)}, s32[768]{0:T(1024)}, u32[]{:S(2)}) copy-start(s32[768]{0:T(1024)} %copy-done.21) | copy-start | bytes 9220
  44.5 48.9 %copy-start.24 = (s32[768]{0:T(1024)S(1)}, s32[768]{0:T(1024)}, u32[]{:S(2)}) copy-start(s32[768]{0:T(1024)} %copy-done.23) | copy-start | bytes 9220
  44.5 48.9 %copy-start.26 = (s32[768]{0:T(1024)S(1)}, s32[768]{0:T(1024)}, u32[]{:S(2)}) copy-start(s32[768]{0:T(1024)} %copy-done.25) | copy-start | bytes 9220
  44.5 48.9 %copy-start.28 = (s32[768]{0:T(1024)S(1)}, s32[768]{0:T(1024)}, u32[]{:S(2)}) copy-start(s32[768]{0:T(1024)} %copy-done.27) | copy-start | bytes 9220
  44.5 48.9 %copy-start.30 = (s32[768]{0:T(1024)S(1)}, s32[768]{0:T(1024)}, u32[]{:S(2)}) copy-start(s32[768]{0:T(1024)} %copy-done.29) | copy-start | bytes 9220
  44.5 48.9 %copy-start.32 = (pred[768]{0:T(1024)(128)(4,1)S(1)}, pred[768]{0:T(1024)(128)(4,1)}, u32[]{:S(2)}) copy-start(pred[768]{0:T(1024)(128)(4,1)} %copy-done.31) | copy-start | bytes 2308
  44.5 48.9 %copy-start.34 = (pred[768]{0:T(1024)(128)(4,1)S(1)}, pred[768]{0:T(1024)(128)(4,1)}, u32[]{:S(2)}) copy-start(pred[768]{0:T(1024)(128)(4,1)} %copy-done.33) | copy-start | bytes 2308
  44.5 48.9 %copy-start.36 = (pred[768]{0:T(1024)(128)(4,1)S(1)}, pred[768]{0:T(1024)(128)(4,1)}, u32[]{:S(2)}) copy-start(pred[768]{0:T(1024)(128)(4,1)} %copy-done.35) | copy-start | bytes 2308
  44.5 48.9 %copy-start.38 = (pred[768]{0:T(1024)(128)(4,1)S(1)}, pred[768]{0:T(1024)(128)(4,1)}, u32[]{:S(2)}) copy-start(pred[768]{0:T(1024)(128)(4,1)} %copy-done.37) | copy-start | bytes 2308
  87.4 37.4 %collective-permute-start.4 = (bf16[640,640]{1,0:T(8,128)(2,1)}, bf16[640,640]{1,0:T(8,128)(2,1)S(1)}, u32[]{:S(2)}, u32[]{:S(2)}) collective-permute-start(bf16[640,640]{1,0:T(8,128)(2,1)} %pad_maximum_fusion.6), channel_id=1, source_target_pairs={{0,64},{64,0},{128,192},{192,128},{1,65},{65,1},{129,193},{193,129... | collective-permute-start | bytes 2457608 | tf_op jit(solution)/shard_map/ppermute | solution.py:103
  90.8 35.6 %copy-start.13 = (bf16[320,640]{1,0:T(8,128)(2,1)S(1)}, bf16[320,640]{1,0:T(8,128)(2,1)}, u32[]{:S(2)}) copy-start(bf16[320,640]{1,0:T(8,128)(2,1)} %get-tuple-element.25) | copy-start | bytes 1228804
  90.9 35.1 %collective-permute-start.7 = (bf16[192,1280]{1,0:T(8,128)(2,1)S(1)}, bf16[192,1280]{1,0:T(8,128)(2,1)S(1)}, u32[]{:S(2)}, u32[]{:S(2)}) collective-permute-start(bf16[192,1280]{1,0:T(8,128)(2,1)S(1)} %convolution_convert_fusion.2), channel_id=1, source_target_pairs={{0,192},{64,128},{128,64},{192,0},{1,193},{65,129},{129,65},{193,1... | collective-permute-start | bytes 1474568 | tf_op jit(solution)/shard_map/ppermute | solution.py:103
  98.5 29.1 %collective-permute-start = (bf16[192,1280]{1,0:T(8,128)(2,1)S(1)}, bf16[192,1280]{1,0:T(8,128)(2,1)}, u32[]{:S(2)}, u32[]{:S(2)}) collective-permute-start(bf16[192,1280]{1,0:T(8,128)(2,1)S(1)} %convolution_convert_fusion.2), channel_id=1, source_target_pairs={{0,2},{2,0},{1,3},{3,1},{4,6},{6,4},{5,7},{7,5},{8,10},{10,8},{9,1... | collective-permute-start | bytes 1474568 | tf_op jit(solution)/shard_map/ppermute | solution.py:103
  99.3 49.5 %collective-permute-start.17 = (bf16[192,1280]{1,0:T(8,128)(2,1)S(1)}, bf16[192,1280]{1,0:T(8,128)(2,1)S(1)}, u32[]{:S(2)}, u32[]{:S(2)}) collective-permute-start(bf16[192,1280]{1,0:T(8,128)(2,1)S(1)} %convolution_convert_fusion.1), channel_id=1, source_target_pairs={{0,2},{2,0},{1,3},{3,1},{4,6},{6,4},{5,7},{7,5},{8,10},{10,8},{9,1... | collective-permute-start | bytes 1474568 | tf_op jit(solution)/shard_map/ppermute | solution.py:103
  124.9 20.0 %collective-permute-start.14 = (bf16[192,1280]{1,0:T(8,128)(2,1)S(1)}, bf16[192,1280]{1,0:T(8,128)(2,1)S(1)}, u32[]{:S(2)}, u32[]{:S(2)}) collective-permute-start(bf16[192,1280]{1,0:T(8,128)(2,1)S(1)} %convolution_convert_fusion.1), channel_id=1, source_target_pairs={{0,192},{64,128},{128,64},{192,0},{1,193},{65,129},{129,65},{193,1... | collective-permute-start | bytes 1474568 | tf_op jit(solution)/shard_map/ppermute | solution.py:103
  126.0 19.2 %collective-permute-start.8 = (bf16[192,1280]{1,0:T(8,128)(2,1)S(1)}, bf16[192,1280]{1,0:T(8,128)(2,1)S(1)}, u32[]{:S(2)}, u32[]{:S(2)}) collective-permute-start(bf16[192,1280]{1,0:T(8,128)(2,1)S(1)} %collective-permute-done.7), channel_id=1, source_target_pairs={{0,2},{2,0},{1,3},{3,1},{4,6},{6,4},{5,7},{7,5},{8,10},{10,8},{9,1... | collective-permute-start | bytes 1474568 | tf_op jit(solution)/shard_map/ppermute | solution.py:103
  128.7 39.1 %collective-permute-start.1 = (bf16[384,1280]{1,0:T(8,128)(2,1)S(1)}, bf16[384,1280]{1,0:T(8,128)(2,1)S(1)}, u32[]{:S(2)}, u32[]{:S(2)}) collective-permute-start(bf16[384,1280]{1,0:T(8,128)(2,1)S(1)} %pad_maximum_fusion.2), channel_id=1, source_target_pairs={{0,1},{1,0},{2,3},{3,2},{4,5},{5,4},{6,7},{7,6},{8,9},{9,8},{10,11... | collective-permute-start | bytes 2949128 | tf_op jit(solution)/shard_map/ppermute | solution.py:103
  144.8 9.6 %copy-start.15 = (bf16[192,1280]{1,0:T(8,128)(2,1)}, bf16[192,1280]{1,0:T(8,128)(2,1)S(1)}, u32[]{:S(2)}) copy-start(bf16[192,1280]{1,0:T(8,128)(2,1)S(1)} %collective-permute-done.14) | copy-start | bytes 1474564
  144.8 9.6 %collective-permute-start.15 = (bf16[192,1280]{1,0:T(8,128)(2,1)S(1)}, bf16[192,1280]{1,0:T(8,128)(2,1)S(1)}, u32[]{:S(2)}, u32[]{:S(2)}) collective-permute-start(bf16[192,1280]{1,0:T(8,128)(2,1)S(1)} %collective-permute-done.14), channel_id=1, source_target_pairs={{0,2},{2,0},{1,3},{3,1},{4,6},{6,4},{5,7},{7,5},{8,10},{10,8},{9,1... | collective-permute-start | bytes 1474568 | tf_op jit(solution)/shard_map/ppermute | solution.py:103
  145.3 14.2 %collective-permute-start.9 = (bf16[384,1280]{1,0:T(8,128)(2,1)S(1)}, bf16[384,1280]{1,0:T(8,128)(2,1)S(1)}, u32[]{:S(2)}, u32[]{:S(2)}) collective-permute-start(bf16[384,1280]{1,0:T(8,128)(2,1)S(1)} %pad_maximum_fusion.3), channel_id=1, source_target_pairs={{0,1},{1,0},{2,3},{3,2},{4,5},{5,4},{6,7},{7,6},{8,9},{9,8},{10,11... | collective-permute-start | bytes 2949128 | tf_op jit(solution)/shard_map/ppermute | solution.py:103
  148.9 35.1 %collective-permute-start.18 = (bf16[384,1280]{1,0:T(8,128)(2,1)S(1)}, bf16[384,1280]{1,0:T(8,128)(2,1)S(1)}, u32[]{:S(2)}, u32[]{:S(2)}) collective-permute-start(bf16[384,1280]{1,0:T(8,128)(2,1)S(1)} %pad_maximum_fusion.5), channel_id=1, source_target_pairs={{0,1},{1,0},{2,3},{3,2},{4,5},{5,4},{6,7},{7,6},{8,9},{9,8},{10,11... | collective-permute-start | bytes 2949128 | tf_op jit(solution)/shard_map/ppermute | solution.py:103
  149.0 10.6 %copy-start.40 = (f32[768,640]{1,0:T(8,128)S(1)}, f32[768,640]{1,0:T(8,128)}, u32[]{:S(2)}) copy-start(f32[768,640]{1,0:T(8,128)} %fusion.92) | copy-start | bytes 5898244
  155.4 81.1 %collective-permute-start.16 = (bf16[384,1280]{1,0:T(8,128)(2,1)}, bf16[384,1280]{1,0:T(8,128)(2,1)}, u32[]{:S(2)}, u32[]{:S(2)}) collective-permute-start(bf16[384,1280]{1,0:T(8,128)(2,1)} %pad_maximum_fusion.4), channel_id=1, source_target_pairs={{0,1},{1,0},{2,3},{3,2},{4,5},{5,4},{6,7},{7,6},{8,9},{9,8},{10,11... | collective-permute-start | bytes 2949128 | tf_op jit(solution)/shard_map/ppermute | solution.py:103
  159.6 5.3 %copy-start.17 = (bf16[768,1280]{1,0:T(8,128)(2,1)}, bf16[768,1280]{1,0:T(8,128)(2,1)S(1)}, u32[]{:S(2)}) copy-start(bf16[768,1280]{1,0:T(8,128)(2,1)S(1)} %constant_dynamic-update-slice_fusion) | copy-start | bytes 5898244
  167.7 19.7 %collective-permute-start.11 = (bf16[384,1280]{1,0:T(8,128)(2,1)S(1)}, bf16[384,1280]{1,0:T(8,128)(2,1)S(1)}, u32[]{:S(2)}, u32[]{:S(2)}) collective-permute-start(bf16[384,1280]{1,0:T(8,128)(2,1)S(1)} %slice.223), channel_id=1, source_target_pairs={{0,1},{1,0},{2,3},{3,2},{4,5},{5,4},{6,7},{7,6},{8,9},{9,8},{10,11... | collective-permute-start | bytes 2949128 | tf_op jit(solution)/shard_map/ppermute | solution.py:103
  174.5 13.6 %collective-permute-start.5 = (bf16[384,1280]{1,0:T(8,128)(2,1)S(1)}, bf16[384,1280]{1,0:T(8,128)(2,1)S(1)}, u32[]{:S(2)}, u32[]{:S(2)}) collective-permute-start(bf16[384,1280]{1,0:T(8,128)(2,1)S(1)} %slice.224), channel_id=1, source_target_pairs={{0,1},{1,0},{2,3},{3,2},{4,5},{5,4},{6,7},{7,6},{8,9},{9,8},{10,11... | collective-permute-start | bytes 2949128 | tf_op jit(solution)/shard_map/ppermute | solution.py:103
  187.6 12.9 %collective-permute-start.12 = (bf16[192,1280]{1,0:T(8,128)(2,1)S(1)}, bf16[192,1280]{1,0:T(8,128)(2,1)S(1)}, u32[]{:S(2)}, u32[]{:S(2)}) collective-permute-start(bf16[192,1280]{1,0:T(8,128)(2,1)S(1)} %slice.225), channel_id=1, source_target_pairs={{0,2},{2,0},{1,3},{3,1},{4,6},{6,4},{5,7},{7,5},{8,10},{10,8},{9,1... | collective-permute-start | bytes 1474568 | tf_op jit(solution)/shard_map/ppermute | solution.py:103
  188.3 22.7 %collective-permute-start.6 = (bf16[192,1280]{1,0:T(8,128)(2,1)S(1)}, bf16[192,1280]{1,0:T(8,128)(2,1)S(1)}, u32[]{:S(2)}, u32[]{:S(2)}) collective-permute-start(bf16[192,1280]{1,0:T(8,128)(2,1)S(1)} %slice.226), channel_id=1, source_target_pairs={{0,2},{2,0},{1,3},{3,1},{4,6},{6,4},{5,7},{7,5},{8,10},{10,8},{9,1... | collective-permute-start | bytes 1474568 | tf_op jit(solution)/shard_map/ppermute | solution.py:103
  200.6 24.1 %collective-permute-start.13 = (bf16[192,1280]{1,0:T(8,128)(2,1)S(1)}, bf16[192,1280]{1,0:T(8,128)(2,1)S(1)}, u32[]{:S(2)}, u32[]{:S(2)}) collective-permute-start(bf16[192,1280]{1,0:T(8,128)(2,1)S(1)} %fusion.38), channel_id=1, source_target_pairs={{0,192},{64,128},{128,64},{192,0},{1,193},{65,129},{129,65},{193,1... | collective-permute-start | bytes 1474568 | tf_op jit(solution)/shard_map/ppermute | solution.py:103
  209.2 27.3 %copy-start.16 = (bf16[192,1280]{1,0:T(8,128)(2,1)S(1)}, bf16[192,1280]{1,0:T(8,128)(2,1)}, u32[]{:S(2)}) copy-start(bf16[192,1280]{1,0:T(8,128)(2,1)} %copy-done.15) | copy-start | bytes 1474564
  226.2 22.1 %all-to-all-start.1 = ((bf16[16,16,1280]{2,1,0:T(8,128)(2,1)}), bf16[16,16,1280]{2,1,0:T(8,128)(2,1)S(1)}, u32[]{:S(2)}, u32[]{:S(2)}) async-start(bf16[16,16,1280]{2,1,0:T(8,128)(2,1)} %bitcast.9), calls=%async_computation.1 | async-start | bytes 1310720 | tf_op jit(solution)/shard_map/all_to_all | solution.py:220
  236.5 8.5 %copy-start.39 = (f32[640,1280]{1,0:T(8,128)S(1)}, f32[640,1280]{1,0:T(8,128)}, u32[]{:S(2)}) copy-start(f32[640,1280]{1,0:T(8,128)} %fusion.37) | copy-start | bytes 9830404
  243.1 5.2 %copy-start.2 = (bf16[12,64,1280]{2,1,0:T(8,128)(2,1)S(1)}, bf16[12,64,1280]{2,1,0:T(8,128)(2,1)}, u32[]{:S(2)}) copy-start(bf16[12,64,1280]{2,1,0:T(8,128)(2,1)} %param.7) | copy-start | bytes 5898244
  243.1 55.4 %collective-permute-start.19 = (bf16[640,640]{1,0:T(8,128)(2,1)}, bf16[640,640]{1,0:T(8,128)(2,1)}, u32[]{:S(2)}, u32[]{:S(2)}) collective-permute-start(bf16[640,640]{1,0:T(8,128)(2,1)} %pad_maximum_fusion.7), channel_id=1, source_target_pairs={{0,64},{64,0},{128,192},{192,128},{1,65},{65,1},{129,193},{193,129... | collective-permute-start | bytes 2457608 | tf_op jit(solution)/shard_map/ppermute | solution.py:103
  250.6 6.8 %copy-start.10 = (f32[640,1280]{1,0:T(8,128)S(1)}, f32[640,1280]{1,0:T(8,128)}, u32[]{:S(2)}) copy-start(f32[640,1280]{1,0:T(8,128)} %convolution_add_fusion) | copy-start | bytes 9830404
  252.5 47.3 %collective-permute-start.22 = (f32[16,1280]{1,0:T(8,128)S(1)}, f32[16,1280]{1,0:T(8,128)S(1)}, u32[]{:S(2)}, u32[]{:S(2)}) collective-permute-start(f32[16,1280]{1,0:T(8,128)S(1)} %get-tuple-element.15), channel_id=1, source_target_pairs={{0,1},{1,0},{2,3},{3,2},{4,5},{5,4},{6,7},{7,6},{8,9},{9,8},{10,11... | collective-permute-start | bytes 245768 | tf_op jit(solution)/shard_map/ppermute | solution.py:103
  255.6 44.2 %collective-permute-start.23 = (f32[16,1280]{1,0:T(8,128)S(1)}, f32[16,1280]{1,0:T(8,128)S(1)}, u32[]{:S(2)}, u32[]{:S(2)}) collective-permute-start(f32[16,1280]{1,0:T(8,128)S(1)} %get-tuple-element.15), channel_id=1, source_target_pairs={{0,2},{1,3},{2,0},{3,1},{4,6},{5,7},{6,4},{7,5},{8,10},{9,11},{10,... | collective-permute-start | bytes 245768 | tf_op jit(solution)/shard_map/ppermute | solution.py:103
  256.1 43.7 %collective-permute-start.24 = (f32[16,1280]{1,0:T(8,128)S(1)}, f32[16,1280]{1,0:T(8,128)S(1)}, u32[]{:S(2)}, u32[]{:S(2)}) collective-permute-start(f32[16,1280]{1,0:T(8,128)S(1)} %get-tuple-element.15), channel_id=1, source_target_pairs={{0,3},{1,2},{2,1},{3,0},{4,7},{5,6},{6,5},{7,4},{8,11},{9,10},{10,... | collective-permute-start | bytes 245768 | tf_op jit(solution)/shard_map/ppermute | solution.py:103
  257.4 46.6 %copy-start.12 = (f32[1280,640]{1,0:T(8,128)S(1)}, f32[1280,640]{1,0:T(8,128)}, u32[]{:S(2)}) copy-start(f32[1280,640]{1,0:T(8,128)} %copy-done.11) | copy-start | bytes 9830404
  257.5 58.5 %collective-permute-start.21 = (bf16[320,1280]{1,0:T(8,128)(2,1)S(1)}, bf16[320,1280]{1,0:T(8,128)(2,1)S(1)}, u32[]{:S(2)}, u32[]{:S(2)}) collective-permute-start(bf16[320,1280]{1,0:T(8,128)(2,1)S(1)} %select_convert_fusion), channel_id=1, source_target_pairs={{0,64},{64,0},{128,192},{192,128},{1,65},{65,1},{129,193},{193,129... | collective-permute-start | bytes 2457608 | tf_op jit(solution)/shard_map/ppermute | solution.py:103
  299.8 4.6 %collective-permute-start.25 = (f32[16,1280]{1,0:T(8,128)S(1)}, f32[16,1280]{1,0:T(8,128)S(1)}, u32[]{:S(2)}, u32[]{:S(2)}) collective-permute-start(f32[16,1280]{1,0:T(8,128)S(1)} %add_add_fusion.2), channel_id=1, source_target_pairs={{0,16},{16,0},{32,48},{48,32},{1,17},{17,1},{33,49},{49,33},{2,18}... | collective-permute-start | bytes 245768 | tf_op jit(solution)/shard_map/ppermute | solution.py:103
  301.4 5.1 %collective-permute-start.26 = (f32[16,1280]{1,0:T(8,128)S(1)}, f32[16,1280]{1,0:T(8,128)S(1)}, u32[]{:S(2)}, u32[]{:S(2)}) collective-permute-start(f32[16,1280]{1,0:T(8,128)S(1)} %add_add_fusion.2), channel_id=1, source_target_pairs={{0,32},{16,48},{32,0},{48,16},{1,33},{17,49},{33,1},{49,17},{2,34}... | collective-permute-start | bytes 245768 | tf_op jit(solution)/shard_map/ppermute | solution.py:103
  303.8 4.6 %collective-permute-start.27 = (f32[16,1280]{1,0:T(8,128)S(1)}, f32[16,1280]{1,0:T(8,128)S(1)}, u32[]{:S(2)}, u32[]{:S(2)}) collective-permute-start(f32[16,1280]{1,0:T(8,128)S(1)} %add_add_fusion.2), channel_id=1, source_target_pairs={{0,48},{16,32},{32,16},{48,0},{1,49},{17,33},{33,17},{49,1},{2,50}... | collective-permute-start | bytes 245768 | tf_op jit(solution)/shard_map/ppermute | solution.py:103
  304.2 33.5 %collective-permute-start.20 = (bf16[320,640]{1,0:T(8,128)(2,1)S(1)}, bf16[320,640]{1,0:T(8,128)(2,1)S(1)}, u32[]{:S(2)}, u32[]{:S(2)}) collective-permute-start(bf16[320,640]{1,0:T(8,128)(2,1)S(1)} %get-tuple-element.17), channel_id=1, source_target_pairs={{0,192},{64,128},{128,64},{192,0},{1,193},{65,129},{129,65},{193,1... | collective-permute-start | bytes 1228808 | tf_op jit(solution)/shard_map/ppermute | solution.py:103
  308.5 8.7 %collective-permute-start.28 = (f32[16,1280]{1,0:T(8,128)S(1)}, f32[16,1280]{1,0:T(8,128)S(1)}, u32[]{:S(2)}, u32[]{:S(2)}) collective-permute-start(f32[16,1280]{1,0:T(8,128)S(1)} %add_add_fusion.1), channel_id=1, source_target_pairs={{0,4},{4,0},{8,12},{12,8},{1,5},{5,1},{9,13},{13,9},{2,6},{6,2},{1... | collective-permute-start | bytes 245768 | tf_op jit(solution)/shard_map/ppermute | solution.py:103
  311.3 16.3 %collective-permute-start.29 = (f32[16,1280]{1,0:T(8,128)S(1)}, f32[16,1280]{1,0:T(8,128)S(1)}, u32[]{:S(2)}, u32[]{:S(2)}) collective-permute-start(f32[16,1280]{1,0:T(8,128)S(1)} %add_add_fusion.1), channel_id=1, source_target_pairs={{0,8},{4,12},{8,0},{12,4},{1,9},{5,13},{9,1},{13,5},{2,10},{6,14},... | collective-permute-start | bytes 245768 | tf_op jit(solution)/shard_map/ppermute | solution.py:103
  313.2 18.7 %collective-permute-start.30 = (f32[16,1280]{1,0:T(8,128)S(1)}, f32[16,1280]{1,0:T(8,128)S(1)}, u32[]{:S(2)}, u32[]{:S(2)}) collective-permute-start(f32[16,1280]{1,0:T(8,128)S(1)} %add_add_fusion.1), channel_id=1, source_target_pairs={{0,12},{4,8},{8,4},{12,0},{1,13},{5,9},{9,5},{13,1},{2,14},{6,10},... | collective-permute-start | bytes 245768 | tf_op jit(solution)/shard_map/ppermute | solution.py:103
  332.0 9.3 %collective-permute-start.31 = (f32[16,1280]{1,0:T(8,128)S(1)}, f32[16,1280]{1,0:T(8,128)S(1)}, u32[]{:S(2)}, u32[]{:S(2)}) collective-permute-start(f32[16,1280]{1,0:T(8,128)S(1)} %add_add_fusion), channel_id=1, source_target_pairs={{0,64},{64,0},{128,192},{192,128},{1,65},{65,1},{129,193},{193,129... | collective-permute-start | bytes 245768 | tf_op jit(solution)/shard_map/ppermute | solution.py:103
  332.1 9.2 %collective-permute-start.32 = (f32[16,1280]{1,0:T(8,128)S(1)}, f32[16,1280]{1,0:T(8,128)S(1)}, u32[]{:S(2)}, u32[]{:S(2)}) collective-permute-start(f32[16,1280]{1,0:T(8,128)S(1)} %add_add_fusion), channel_id=1, source_target_pairs={{0,128},{64,192},{128,0},{192,64},{1,129},{65,193},{129,1},{193,65... | collective-permute-start | bytes 245768 | tf_op jit(solution)/shard_map/ppermute | solution.py:103
  335.1 9.8 %collective-permute-start.33 = (f32[16,1280]{1,0:T(8,128)S(1)}, f32[16,1280]{1,0:T(8,128)S(1)}, u32[]{:S(2)}, u32[]{:S(2)}) collective-permute-start(f32[16,1280]{1,0:T(8,128)S(1)} %add_add_fusion), channel_id=1, source_target_pairs={{0,192},{64,128},{128,64},{192,0},{1,193},{65,129},{129,65},{193,1... | collective-permute-start | bytes 245768 | tf_op jit(solution)/shard_map/ppermute | solution.py:103
  (17 other events, 41.9 us)
